TPU v7x, 32 devices: a whole 2x2x4 slice. The times are simulated.
32 devices in a mesh: grp: 2 (over y), blk: 4 (over z), fac: 4 (over x, core).
Axes of the slice: x: 2, y: 2, z: 4, core: 2. Of those that a mesh axis runs over, the one named last changes fastest.
Arguments:
- train_grads: bfloat16 [4096, 8192], P(('grp', 'blk')), parts along dimension 0, may hold values from -0.0625 to 0.0625
- queries: bfloat16 [2048, 8192], P(('grp', 'fac'), 'blk'), parts along dimension 0, may hold values from -6 to 6
- factor: bfloat16 [8192, 8192], P('blk', 'fac'), may hold values from -0.0625 to 0.0625
Outputs:
- scores: float32 [4096, 1024], P(('grp', 'blk'), 'fac'), parts along dimension 0
There are 2 independent parts, one for each index of `grp`. A program takes and returns all parts, laid end to end along the dimension named above; an argument that names none is the same for every part. Nothing has to cross between parts.
All inputs are finite; a program needn't handle non-finite values.
Results may differ from a plain program's by a relative error of at most 0.009.
Values may be sent and summed in bfloat16 or wider, within the bound.
A program may use at most 128 MiB of HBM per device.

v0:
```python
import jax
import jax.numpy as jnp
from jax import lax
from jax.sharding import PartitionSpec as P


def passed_along(value, axis, steps):
    count = lax.axis_size(axis)
    pairs = [(source, (source + steps) % count) for source in range(count)]
    return lax.ppermute(value, axis, pairs)


def contract_last(left, right):
    return lax.dot_general(
        left, right, (((1,), (1,)), ((), ())), preferred_element_type=jnp.float32
    )


def contract_cross(left, right):
    return lax.dot_general(
        left, right, (((0,), (1,)), ((), ())), preferred_element_type=jnp.float32
    )


def shards(train_grads, queries, factor):
    factor_rows = lax.all_gather(factor, "fac", axis=1, tiled=True)
    mixed_rows = contract_last(
        lax.all_gather(queries, "blk", axis=1, tiled=True), factor_rows
    ).astype(jnp.bfloat16)
    members = lax.axis_size("blk")
    dim_share = factor_rows.shape[1] // members
    panel = lax.psum_scatter(
        contract_cross(factor_rows, mixed_rows).astype(jnp.bfloat16),
        "blk",
        scatter_dimension=0,
        tiled=True,
    )
    position = lax.axis_index("blk")

    def score_tile(results, current, rounds):
        source = (position - rounds) % members
        grad_slab = lax.dynamic_slice_in_dim(train_grads, source * dim_share, dim_share, 1)
        return results + jnp.dot(grad_slab, current, preferred_element_type=jnp.float32)

    def advance(rounds, state):
        results, current = state
        results = score_tile(results, current, rounds)
        current = passed_along(current, "blk", 1)
        return (results, current)

    results = jnp.zeros((train_grads.shape[0], mixed_rows.shape[0]), jnp.float32)
    results, panel = lax.fori_loop(0, members - 1, advance, (results, panel))
    return score_tile(results, panel, members - 1)


def solution(mesh):
    placed = (P(("grp", "blk"), None), P(("grp", "fac"), "blk"), P("blk", "fac"))
    return jax.shard_map(
        shards, mesh=mesh, in_specs=placed, out_specs=P(("grp", "blk"), "fac"), check_vma=False
    )
```

profile of v0, /device:TPU:0, one launch (start us, length us, event | category | flops | bytes accessed | tf_op | source)
XLA Modules:
  0.0 492.1 jit_solution(11564468441163970148)
XLA Ops:
  6.5 0.0 all-gather.3.cloned.1.call-start
  6.5 0.7 all-gather.3.cloned.1.call-update
  7.3 0.0 all-gather.5.cloned.1.call-start
  7.3 0.7 all-gather.5.cloned.1.call-update
  8.0 0.0 reduce-scatter.2.cloned.1.call-start
  8.1 84.4 %all-gather.3.cloned.1.call-done = bf16[256,8192]{1,0:T(8,128)(2,1)} async-done(((bf16[256,2048]{1,0:T(8,128)(2,1)}), bf16[256,8192]{1,0:T(8,128)(2,1)}) %all-gather.3.cloned.1.call-update) | async-done | bytes 4194320 | tf_op jit(solution)/shard_map/all_gather | solution.py:28
  92.4 201.7 %all-gather.5.cloned.1.call-done = bf16[2048,8192]{1,0:T(8,128)(2,1)} async-done(((bf16[2048,2048]{1,0:T(8,128)(2,1)}), bf16[2048,8192]{1,0:T(8,128)(2,1)}) %all-gather.5.cloned.1.call-update) | async-done | bytes 33554448 | tf_op jit(solution)/shard_map/all_gather | solution.py:26
  294.1 15.7 %convolution_convert_fusion.1.clone.4 = bf16[256,2048]{1,0:T(8,128)(2,1)S(1)} fusion(bf16[256,8192]{1,0:T(8,128)(2,1)} %all-gather.3.cloned.1.call-done, bf16[2048,8192]{1,0:T(8,128)(2,1)} %all-gather.5.cloned.1.call-done), kind=kOutput, calls=%fused_computation.6.clone.clone.clone.1 | convolution fusion | flops 8590458880 | bytes 38797312 | tf_op jit(solution)/shard_map/dot_general | solution.py:14
  309.8 16.4 %fusion.6 = bf16[8192,256]{0,1:T(8,128)(2,1)} fusion(bf16[2048,8192]{1,0:T(8,128)(2,1)} %all-gather.5.cloned.1.call-done, bf16[256,2048]{1,0:T(8,128)(2,1)S(1)} %convolution_convert_fusion.1.clone.4), kind=kOutput, calls=%fused_computation.5 | convolution fusion | flops 8592031744 | bytes 38797312 | tf_op jit(solution)/shard_map/dot_general | solution.py:20
  326.2 0.0 reduce-scatter.2.cloned.1.call-update
  326.2 76.9 %reduce-scatter.2.cloned.1.call-done = bf16[2048,256]{0,1:T(8,128)(2,1)} async-done(((bf16[8192,256]{0,1:T(8,128)(2,1)}), bf16[2048,256]{0,1:T(8,128)(2,1)}) %reduce-scatter.2.cloned.1.call-update) | async-done | bytes 1048592 | tf_op jit(solution)/shard_map/reduce_scatter | solution.py:32
  403.1 1.5 copy.4
  404.6 77.9 %while.18 = (s32[]{:T(128)}, f32[512,256]{1,0:T(8,128)S(1)}, bf16[2048,256]{1,0:T(8,128)(2,1)S(1)}, s32[]{:T(128)}, bf16[512,8192]{1,0:T(8,128)(2,1)}, /*index=5...) while((s32[]{:T(128)}, f32[512,256]{1,0:T(8,128)S(1)}, ...), condition=%wide.region_2.3_spmd.clone, body=%wide.region_1.2_spmd.clone.sunk | while | flops 537133056 | bytes 10486090 | solution.py:52
  404.6 0.1 copy.10
  404.7 1.5 collective-permute-start
  406.2 2.4 fusion.31
  408.7 22.8 %collective-permute-done = bf16[2048,256]{1,0:T(8,128)(2,1)S(1)} collective-permute-done((bf16[2048,256]{1,0:T(8,128)(2,1)S(1)}, bf16[2048,256]{1,0:T(8,128)(2,1)S(1)}, u32[]{:S(2)}, u32[]{:S(2)}) %collective-permute-start) | collective-permute-done | bytes 1048608 | tf_op jit(solution)/shard_map/while/body/eval_jaxpr/ppermute | solution.py:10
  431.5 0.1 copy.10
  431.5 0.1 collective-permute-start
  431.6 2.4 fusion.31
  434.1 23.4 %collective-permute-done = bf16[2048,256]{1,0:T(8,128)(2,1)S(1)} collective-permute-done((bf16[2048,256]{1,0:T(8,128)(2,1)S(1)}, bf16[2048,256]{1,0:T(8,128)(2,1)S(1)}, u32[]{:S(2)}, u32[]{:S(2)}) %collective-permute-start) | collective-permute-done | bytes 1048608 | tf_op jit(solution)/shard_map/while/body/eval_jaxpr/ppermute | solution.py:10
  457.4 0.1 copy.10
  457.5 0.1 collective-permute-start
  457.6 2.4 fusion.31
  460.1 22.4 %collective-permute-done = bf16[2048,256]{1,0:T(8,128)(2,1)S(1)} collective-permute-done((bf16[2048,256]{1,0:T(8,128)(2,1)S(1)}, bf16[2048,256]{1,0:T(8,128)(2,1)S(1)}, u32[]{:S(2)}, u32[]{:S(2)}) %collective-permute-start) | collective-permute-done | bytes 1048608 | tf_op jit(solution)/shard_map/while/body/eval_jaxpr/ppermute | solution.py:10
  482.5 3.1 fusion.9
  (1 shorter events, 0.0 us)
Async XLA Ops:
  6.5 85.9 %all-gather.3.cloned.1.call-start = ((), (), s32[]{:S(2)}) async-start(), calls=%async_computation.1 | async-start | bytes 5242880 | tf_op jit(solution)/shard_map/all_gather | solution.py:28
  7.3 286.8 %all-gather.5.cloned.1.call-start = ((), (), s32[]{:S(2)}) async-start(), calls=%async_computation.2 | async-start | bytes 41943040 | tf_op jit(solution)/shard_map/all_gather | solution.py:26
  8.0 395.1 %reduce-scatter.2.cloned.1.call-start = ((), (), s32[]{:S(2)}) async-start(), calls=%async_computation.3 | async-start | bytes 5242880 | tf_op jit(solution)/shard_map/reduce_scatter | solution.py:32
  404.7 26.8 %collective-permute-start = (bf16[2048,256]{1,0:T(8,128)(2,1)S(1)}, bf16[2048,256]{1,0:T(8,128)(2,1)S(1)}, u32[]{:S(2)}, u32[]{:S(2)}) collective-permute-start(bf16[2048,256]{1,0:T(8,128)(2,1)S(1)} %copy.10), channel_id=1, source_target_pairs={{0,4},{4,8},{8,12},{12,0},{1,5},{5,9},{9,13},{13,1},{2,6},{6,10},{... | collective-permute-start | bytes 3145736 | tf_op jit(solution)/shard_map/while/body/eval_jaxpr/ppermute | solution.py:10
  431.5 25.9 %collective-permute-start = (bf16[2048,256]{1,0:T(8,128)(2,1)S(1)}, bf16[2048,256]{1,0:T(8,128)(2,1)S(1)}, u32[]{:S(2)}, u32[]{:S(2)}) collective-permute-start(bf16[2048,256]{1,0:T(8,128)(2,1)S(1)} %copy.10), channel_id=1, source_target_pairs={{0,4},{4,8},{8,12},{12,0},{1,5},{5,9},{9,13},{13,1},{2,6},{6,10},{... | collective-permute-start | bytes 3145736 | tf_op jit(solution)/shard_map/while/body/eval_jaxpr/ppermute | solution.py:10
  457.5 25.0 %collective-permute-start = (bf16[2048,256]{1,0:T(8,128)(2,1)S(1)}, bf16[2048,256]{1,0:T(8,128)(2,1)S(1)}, u32[]{:S(2)}, u32[]{:S(2)}) collective-permute-start(bf16[2048,256]{1,0:T(8,128)(2,1)S(1)} %copy.10), channel_id=1, source_target_pairs={{0,4},{4,8},{8,12},{12,0},{1,5},{5,9},{9,13},{13,1},{2,6},{6,10},{... | collective-permute-start | bytes 3145736 | tf_op jit(solution)/shard_map/while/body/eval_jaxpr/ppermute | solution.py:10
Sparse Core Ops, SparseCore 0:
  8.9 83.4 all-gather.2
  94.0 200.0 all-gather.4
  326.3 76.7 reduce-scatter.1
where the time goes:
time: 492 us
  waiting for transfers between devices  433 us (88%)
  matrix products  42.5 us (9%)
  between operations  13.2 us (3%)
    all_gather x1, waiting for transfers between devices, shards(): factor_rows = lax.all_gather(factor, 'fac', axis=1, tiled=True)  202 us
    all_gather x1, waiting for transfers between devices, shards(): lax.all_gather(queries, 'blk', axis=1, tiled=True)  84.4 us
    reduce_scatter x1, waiting for transfers between devices, shards(): lax.psum_scatter(contract_cross(factor_rows, mixed_rows).astype(jnp.bfloa...  76.9 us
    ppermute x3, waiting for transfers between devices, passed_along(): return lax.ppermute(value, axis, pairs)  68.6 us
    dot_general x1, matrix products, contract_cross(): lax.dot_general(left, right, (((0,), (1,)), ((), ())), preferred_element_...  16.4 us
    dot_general x1, matrix products, contract_last(): lax.dot_general(left, right, (((1,), (1,)), ((), ())), preferred_element_...  15.7 us
    dot_general x4, matrix products, score_tile(): jnp.dot(grad_slab, current, preferred_element_type=jnp.float32)  10.4 us
  transfers between devices with their start and end apart: 6, of which 6 were waited for; matrix products, arithmetic and copies ran while one was open for 1% of the time, Pallas kernels for 0%

commit v1 on v0

v1 whole, which is shorter than its diff:
```python
import functools

import jax
import jax.numpy as jnp
from jax import lax
from jax.experimental import pallas as pl
from jax.experimental.pallas import tpu as pltpu
from jax.sharding import PartitionSpec as P

MESH = pl.DeviceIdType.MESH
CORES = 2
STEP_ROWS = 128
TILE_ROWS = 256
HOP = 2
CHUNK = 128

contract_last = functools.partial(
    lax.dot_general,
    dimension_numbers=(((1,), (1,)), ((), ())),
    preferred_element_type=jnp.float32,
)


def at_multiple(start, size):
    return pl.ds(pl.multiple_of(start, size), size)


def remote(src, dst, sems, index, target):
    send_sems, recv_sems = sems
    return pltpu.make_async_remote_copy(
        src_ref=src,
        dst_ref=dst,
        send_sem=send_sems.at[index],
        recv_sem=recv_sems.at[index],
        device_id=target,
        device_id_type=MESH,
    )


def meet(targets):
    barrier = pltpu.get_barrier_semaphore()
    for target in targets:
        pl.semaphore_signal(barrier, inc=1, device_id=target, device_id_type=MESH)
    pl.semaphore_wait(barrier, len(targets))


def term_kernel(
    n_blk, n_fac, queries, factor, term, all_queries, rows, total,
    local_sems, q_send, q_recv, x_send, x_recv, y_send, y_recv, o_send, o_recv, c_send, c_recv,
):
    grp, blk, fac = lax.axis_index("grp"), lax.axis_index("blk"), lax.axis_index("fac")
    chips = n_fac // CORES
    chip, core = fac // CORES, fac % CORES
    n_rows, width = factor.shape
    q_width = queries.shape[1]
    steps, half = n_rows // STEP_ROWS, STEP_ROWS // 2
    q_sems, x_sems, y_sems, o_sems, c_sems = (
        (q_send, q_recv), (x_send, x_recv), (y_send, y_recv), (o_send, o_recv), (c_send, c_recv)
    )

    def other_chip(distance):
        return (chip + distance + chips) % chips * CORES + core

    across = {"grp": 1 - grp}
    beside = {"fac": chip * CORES + 1 - core}
    meet(
        [across, beside]
        + [{"fac": other_chip(distance)} for distance in range(1, chips)]
        + [{"blk": (blk + 1) % n_blk}, {"blk": (blk + n_blk - 1) % n_blk}]
    )

    def region(start, size, owner):
        return rows.at[at_multiple(start, size), at_multiple(owner * width, width)]

    def own_half(step):
        return step * STEP_ROWS + grp * half

    def x_copy(step, distance, source):
        start = own_half(step)
        return remote(
            factor.at[at_multiple(start, half), :],
            region(start, half, source),
            x_sems,
            (distance - 1) * steps + step,
            {"fac": other_chip(distance)},
        )

    def y_copy(step, distance, which):
        part = region(step * STEP_ROWS + which * half, half, other_chip(-distance))
        return remote(part, part, y_sems, (distance - 1) * steps + step, across)

    def o_copy(step, owner):
        start = step * STEP_ROWS
        return remote(
            factor.at[at_multiple(start, STEP_ROWS), :],
            region(start, STEP_ROWS, owner),
            o_sems,
            step,
            beside,
        )

    def c_copy(step, distance, owner):
        part = region(step * STEP_ROWS, STEP_ROWS, owner)
        return remote(part, part, c_sems, (distance - 1) * steps + step, beside)

    def q_part(owner):
        return all_queries.at[:, at_multiple(owner * q_width, q_width)]

    def q_copy(owner, up):
        to = blk + 1 if up else blk - 1
        src = q_part(owner)
        return remote(src, src, q_sems, owner, {"blk": to})

    def q_send_own(up):
        to = blk + 1 if up else blk - 1
        return pltpu.make_async_remote_copy(
            src_ref=queries,
            dst_ref=q_part(blk),
            send_sem=q_send.at[n_blk if up else n_blk + 1],
            recv_sem=q_recv.at[blk],
            device_id={"blk": to},
            device_id_type=MESH,
        )

    keep_rows = pltpu.make_async_copy(factor, region(0, n_rows, fac), local_sems.at[0])
    keep_queries = pltpu.make_async_copy(queries, q_part(blk), local_sems.at[1])

    pl.when(blk < n_blk - 1)(lambda: q_send_own(True).start())
    pl.when(blk > 0)(lambda: q_send_own(False).start())
    ahead = min(3, steps)
    for step in range(ahead):
        for distance in range(1, chips):
            x_copy(step, distance, fac).start()
    keep_queries.start()
    keep_rows.start()

    def relay_queries(far):
        @pl.when(blk - far >= 0)
        def _():
            q_copy(blk - far, True).wait_recv()
            pl.when(blk < n_blk - 1)(lambda: q_copy(blk - far, True).start())

        @pl.when(blk + far <= n_blk - 1)
        def _():
            q_copy(blk + far, False).wait_recv()
            pl.when(blk > 0)(lambda: q_copy(blk + far, False).start())

    def multiply(tile, first, last):
        here = at_multiple(tile * TILE_ROWS, TILE_ROWS)
        depth = all_queries.shape[1]
        piece = min(2048, depth)

        def part(k, sums):
            cols = at_multiple(k * piece, piece)
            return sums + contract_last(all_queries[:, cols], rows[here, cols])

        zero = jnp.zeros((all_queries.shape[0], TILE_ROWS), jnp.float32)
        mixed = lax.fori_loop(0, depth // piece, part, zero).astype(jnp.bfloat16)
        wide = min(1024, depth)

        @pl.loop(0, depth // wide)
        def _(k):
            cols = at_multiple(k * wide, wide)
            sums = jnp.dot(mixed, rows[here, cols], preferred_element_type=jnp.float32)
            if not first:
                sums = sums + total[:, cols]
            if last:
                term[:, cols] = sums.astype(term.dtype)
            else:
                total[:, cols] = sums

    tiles, per_tile = n_rows // TILE_ROWS, TILE_ROWS // STEP_ROWS
    turns = steps + 2
    begin = turns * 3 // 4 - 1
    done = 0
    for turn in range(turns):
        if turn < steps:
            o_copy(turn, fac).start()
            for distance in range(1, chips):
                x_copy(turn, distance, other_chip(-distance)).wait_recv()
                y_copy(turn, distance, grp).start()
        if 1 <= turn <= steps:
            for distance in range(1, chips):
                y_copy(turn - 1, distance, 1 - grp).wait_recv()
                c_copy(turn - 1, distance, other_chip(-distance)).start()
        if turn < steps:
            for distance in range(1, chips):
                x_copy(turn, distance, fac).wait_send()
                if turn + ahead < steps:
                    x_copy(turn + ahead, distance, fac).start()
        for far in range(1, n_blk):
            if far * begin // (n_blk - 1) == turn:
                relay_queries(far)
        if turn == begin:
            keep_queries.wait()
            keep_rows.wait()
        if turn >= begin:
            allowed = tiles if turn == turns - 1 else min(done + 2, (turn - 1) // per_tile, tiles)
            while done < allowed:
                for step in range(done * per_tile, (done + 1) * per_tile):
                    o_copy(step, fac + 1 - 2 * core).wait_recv()
                    for distance in range(1, chips):
                        c_copy(step, distance, other_chip(-distance) + 1 - 2 * core).wait_recv()
                multiply(done, done == 0, done == tiles - 1)
                done += 1

    pl.when(blk < n_blk - 1)(lambda: q_send_own(True).wait_send())
    pl.when(blk > 0)(lambda: q_send_own(False).wait_send())
    for far in range(1, n_blk):
        pl.when((blk - far >= 0) & (blk < n_blk - 1))(lambda: q_copy(blk - far, True).wait_send())
        pl.when((blk + far <= n_blk - 1) & (blk > 0))(lambda: q_copy(blk + far, False).wait_send())
    for step in range(steps):
        o_copy(step, fac).wait_send()
        for distance in range(1, chips):
            y_copy(step, distance, grp).wait_send()
            c_copy(step, distance, other_chip(-distance)).wait_send()


def term_of(queries, factor, n_blk, n_fac):
    n_queries, n_rows = queries.shape[0], factor.shape[0]
    dims = factor.shape[1] * n_fac
    steps = n_rows // STEP_ROWS
    far_steps = steps * (n_fac // CORES - 1)
    dma = pltpu.SemaphoreType.DMA
    pairs = [far_steps] * 4 + [steps] * 2 + [far_steps] * 2
    return pl.pallas_call(
        functools.partial(term_kernel, n_blk, n_fac),
        out_shape=jax.ShapeDtypeStruct((n_queries, dims), jnp.bfloat16),
        in_specs=[pl.BlockSpec(memory_space=pl.ANY)] * 2,
        out_specs=pl.BlockSpec(memory_space=pltpu.VMEM),
        scratch_shapes=[
            pltpu.VMEM((n_queries, dims), jnp.bfloat16),
            pltpu.VMEM((n_rows, dims), jnp.bfloat16),
            pltpu.VMEM((n_queries, dims), jnp.float32),
            dma((2,)),
            dma((n_blk + 2,)),
            dma((n_blk,)),
        ]
        + [dma((count,)) for count in pairs],
        compiler_params=pltpu.CompilerParams(
            collective_id=0, has_side_effects=True, vmem_limit_bytes=56 * 2**20
        ),
    )(queries, factor)


def score_kernel(n_blk, term, train, scores, sums, precond, grads, load_sem, *sems):
    blk = lax.axis_index("blk")
    dims = term.shape[1]
    count = dims // 2 // CHUNK
    up_sum, down_sum, up_share, down_share = (
        (sems[2 * k], sems[2 * k + 1]) for k in range(4)
    )
    meet([{"blk": (blk + 1) % n_blk}, {"blk": (blk + n_blk - 1) % n_blk}])
    load = pltpu.make_async_copy(train, grads, load_sem)
    load.start()
    scores[...] = jnp.zeros_like(scores)

    flows = (
        (blk, {"blk": blk + 1}, {"blk": blk - 1}, 0, up_sum, up_share),
        (n_blk - 1 - blk, {"blk": blk - 1}, {"blk": blk + 1}, dims // 2, down_sum, down_share),
    )
    last = n_blk - 1

    def chunk(base, i):
        return (slice(None), at_multiple(base + i * CHUNK, CHUNK))

    def sum_copy(flow, i, first=False):
        _, ahead, _, base, sum_sems, _ = flow
        here = chunk(base, i)
        return remote((term if first else sums).at[here], sums.at[here], sum_sems, i, ahead)

    def share_copy(flow, i):
        _, _, back, base, _, share_sems = flow
        part = precond.at[chunk(base, i)]
        return remote(part, part, share_sems, i, back)

    def add(flow, i):
        place, base = flow[0], flow[3]
        here = chunk(base, i)

        @pl.when(place == 0)
        def _():
            sum_copy(flow, i, True).start()

        @pl.when(place > 0)
        def _():
            sum_copy(flow, i).wait_recv()
            added = sums[here].astype(jnp.float32) + term[here].astype(jnp.float32)
            added = added.astype(jnp.bfloat16)

            @pl.when(place < last)
            def _():
                sums[here] = added
                sum_copy(flow, i).start()

            @pl.when(place == last)
            def _():
                precond[here] = added
                share_copy(flow, i).start()

    def use(flow, i):
        place, base = flow[0], flow[3]

        @pl.when(place < last)
        def _():
            share_copy(flow, i).wait_recv()
            pl.when(place > 0)(lambda: share_copy(flow, i).start())

        @pl.when(i % 2 == 1)
        def _():
            cols = at_multiple(base + (i // 2) * (2 * CHUNK), 2 * CHUNK)
            scores[...] += contract_last(grads[:, cols], precond[:, cols])

    def turn(t, with_use):
        for flow in flows:
            i = t - flow[0] * HOP
            pl.when((i >= 0) & (i < count))(functools.partial(add, flow, i))
        if with_use:
            for flow in flows:
                i = t - (2 * last - flow[0]) * HOP
                pl.when((i >= 0) & (i < count))(functools.partial(use, flow, i))

    @pl.loop(0, last * HOP)
    def _(t):
        turn(t, False)

    load.wait()

    @pl.loop(last * HOP, count + 2 * last * HOP)
    def _(t):
        turn(t, True)

    for flow in flows:
        place = flow[0]

        @pl.loop(0, count)
        def _(i):
            pl.when(place < last)(lambda: sum_copy(flow, i).wait_send())
            pl.when(place > 0)(lambda: share_copy(flow, i).wait_send())


def scores_of(term, train, n_blk):
    dma = pltpu.SemaphoreType.DMA
    count = term.shape[1] // 2 // CHUNK
    return pl.pallas_call(
        functools.partial(score_kernel, n_blk),
        out_shape=jax.ShapeDtypeStruct((train.shape[0], term.shape[0]), jnp.float32),
        in_specs=[pl.BlockSpec(memory_space=pltpu.VMEM), pl.BlockSpec(memory_space=pl.ANY)],
        out_specs=pl.BlockSpec(memory_space=pltpu.VMEM),
        scratch_shapes=[
            pltpu.VMEM(term.shape, jnp.bfloat16),
            pltpu.VMEM(term.shape, jnp.bfloat16),
            pltpu.VMEM(train.shape, jnp.bfloat16),
            dma(()),
        ]
        + [dma((count,))] * 8,
        compiler_params=pltpu.CompilerParams(
            collective_id=1, has_side_effects=True, vmem_limit_bytes=48 * 2**20
        ),
    )(term, train)


def solution(mesh):
    n_blk, n_fac = mesh.shape["blk"], mesh.shape["fac"]

    def shards(train_grads, queries, factor):
        term = term_of(queries, factor, n_blk, n_fac)
        return scores_of(term, train_grads, n_blk)

    placed = (P(("grp", "blk"), None), P(("grp", "fac"), "blk"), P("blk", "fac"))
    return jax.shard_map(
        shards, mesh=mesh, in_specs=placed, out_specs=P(("grp", "blk"), "fac"), check_vma=False
    )
```

time: 492 us -> 233 us (0.47)
  waiting for transfers between devices: 433 us -> 0 us
  Pallas kernels: 0 us -> 229 us
  matrix products: 42.5 us -> 0 us
  between operations: 13.2 us -> 0.03 us
    all_gather x2 -> x0, waiting for transfers between devices: 286 us -> none  [the longest x1 202 us: shards(): factor_rows = lax.all_gather(factor, 'fac', axis=1, tiled=True)]
    pallas_call x0 -> x2, Pallas kernels: none -> 229 us  [the longest x1 121 us: term_of(): pl.pallas_call(functools.partial(term_kernel, n_blk, n_fac), out_shape=ja...]
    reduce_scatter x1 -> x0, waiting for transfers between devices: 76.9 us -> none  [shards(): lax.psum_scatter(contract_cross(factor_rows, mixed_rows).astype(jnp.bfloa...]
    ppermute x3 -> x0, waiting for transfers between devices: 68.6 us -> none  [passed_along(): return lax.ppermute(value, axis, pairs)]
    dot_general x6 -> x0, matrix products: 42.5 us -> none  [the longest x1 16.4 us: contract_cross(): lax.dot_general(left, right, (((0,), (1,)), ((), ())), preferred_element_...]
  transfers between devices with their start and end apart: 6 -> 0, of which waited for: 6 -> 0; matrix products, arithmetic and copies ran while one was open for 1% -> 0% of each run, Pallas kernels for 0% -> 0%
where the time goes in v1:
time: 233 us; the launch traced here: 232 us
  Pallas kernels  229 us (98%)
  local copies, waits for them, and re-layouts  2.98 us (1%)
    pallas_call x1, Pallas kernels, term_of(): pl.pallas_call(functools.partial(term_kernel, n_blk, n_fac), out_shape=ja...  121 us
    pallas_call x1, Pallas kernels, scores_of(): pl.pallas_call(functools.partial(score_kernel, n_blk), out_shape=jax.Shap...  108 us

profile of v1, /device:TPU:0, one launch (start us, length us, event | category | flops | bytes accessed | tf_op | source)
XLA Modules:
  0.0 232.4 jit_solution(16586807968017074903)
XLA Ops:
  0.0 121.2 %shard_map.37.term = bf16[256,8192]{1,0:T(8,128)(2,1)} custom-call(bf16[256,2048]{1,0:T(8,128)(2,1)} %queries.1, bf16[2048,2048]{1,0:T(8,128)(2,1)} %factor.1), custom_call_target="tpu_custom_call" | custom-call | tf_op jit(solution)/shard_map/pallas_call | solution.py:226
  121.2 0.0 copy-start
  121.3 2.2 copy-done
  123.4 108.1 %shard_map.38 = f32[512,256]{1,0:T(8,128)S(1)} custom-call(bf16[256,8192]{1,0:T(8,128)(2,1)S(1)} %copy-done, bf16[512,8192]{1,0:T(8,128)(2,1)} %train.1), custom_call_target="tpu_custom_call" | custom-call | tf_op jit(solution)/shard_map/pallas_call | solution.py:345
  231.6 0.8 copy.5
Async XLA Ops:
  121.2 2.2 copy-start

commit v2 on v0

v2 whole, which is shorter than its diff:
```python
import functools

import jax
import jax.numpy as jnp
from jax import lax
from jax.experimental import pallas as pl
from jax.experimental.pallas import tpu as pltpu
from jax.sharding import PartitionSpec as P

MESH = pl.DeviceIdType.MESH
CORES = 2
SLABS = 4
HOP = 2
CHUNK = 256

contract_last = functools.partial(
    lax.dot_general,
    dimension_numbers=(((1,), (1,)), ((), ())),
    preferred_element_type=jnp.float32,
)


def at_multiple(start, size):
    return pl.ds(pl.multiple_of(start, size), size)


def remote(src, dst, sems, index, target):
    send_sems, recv_sems = sems
    return pltpu.make_async_remote_copy(
        src_ref=src,
        dst_ref=dst,
        send_sem=send_sems.at[index],
        recv_sem=recv_sems.at[index],
        device_id=target,
        device_id_type=MESH,
    )


def meet(targets):
    barrier = pltpu.get_barrier_semaphore()
    for target in targets:
        pl.semaphore_signal(barrier, inc=1, device_id=target, device_id_type=MESH)
    pl.semaphore_wait(barrier, len(targets))


def kernel(
    n_blk, n_fac, train, queries, factor, scores,
    weights, whole, mixing, partial, arrived, mixed, term, sums, precond, grads, found, others,
    gathered, local_sems, *sems,
):
    blk, fac = lax.axis_index("blk"), lax.axis_index("fac")
    chips = n_fac // CORES
    chip, core = fac // CORES, fac % CORES
    n_rows, width = factor.shape
    n_queries, q_width = queries.shape
    span = CORES * width
    share = n_queries // SLABS
    slab = chips * share
    pairs = [(sems[2 * k], sems[2 * k + 1]) for k in range(len(sems) // 2)]
    q_sems, f_sems, a_sems, b_sems, s_sems, up_sum, down_sum, up_share, down_share = pairs
    last = n_blk - 1

    def other_chip(distance):
        return (chip + distance + chips) % chips

    def device_of(place):
        return {"fac": place * CORES + core}

    beside = {"fac": chip * CORES + 1 - core}
    far_chips = range(1, chips)
    meet(
        [beside]
        + [device_of(other_chip(distance)) for distance in far_chips]
        + [{"blk": (blk + 1) % n_blk}, {"blk": (blk + last) % n_blk}]
    )

    def q_part(owner, k):
        return whole.at[at_multiple(k * share, share), at_multiple(owner * q_width, q_width)]

    def q_own(k, up):
        return pltpu.make_async_remote_copy(
            src_ref=queries.at[at_multiple(k * share, share), :],
            dst_ref=q_part(blk, k),
            send_sem=q_sems[0].at[(n_blk if up else n_blk + 1) * SLABS + k],
            recv_sem=q_sems[1].at[blk * SLABS + k],
            device_id={"blk": blk + 1 if up else blk - 1},
            device_id_type=MESH,
        )

    def q_relay(owner, k, up):
        part = q_part(owner, k)
        return remote(part, part, q_sems, owner * SLABS + k, {"blk": blk + 1 if up else blk - 1})

    def own_queries(k):
        pl.when(blk < last)(lambda: q_own(k, True).start())
        pl.when(blk > 0)(lambda: q_own(k, False).start())

    def relay(k, far):
        @pl.when(blk - far >= 0)
        def _():
            q_relay(blk - far, k, True).wait_recv()
            pl.when(blk < last)(lambda: q_relay(blk - far, k, True).start())

        @pl.when(blk + far <= last)
        def _():
            q_relay(blk + far, k, False).wait_recv()
            pl.when(blk > 0)(lambda: q_relay(blk + far, k, False).start())

    def columns_of(owner_core):
        return weights.at[:, at_multiple(owner_core * width, width)]

    def f_copy(owner_core):
        return remote(factor, columns_of(owner_core), f_sems, 0, beside)

    def a_copy(k, distance, source):
        to = other_chip(distance)
        return remote(
            whole.at[at_multiple(k * share, share), at_multiple(to * span, span)],
            mixing.at[at_multiple(k * slab + source * share, share), :],
            a_sems,
            (distance - 1) * SLABS + k,
            device_of(to),
        )

    def b_copy(k, distance):
        here = at_multiple(k * slab, slab)
        return remote(
            partial.at[here, :],
            arrived.at[distance - 1, here, :],
            b_sems,
            (distance - 1) * SLABS + k,
            device_of(other_chip(distance)),
        )

    def s_copy(k, distance):
        to = other_chip(distance)
        return remote(
            found.at[at_multiple(k * slab + to * share, share), :],
            others.at[distance - 1, at_multiple(k * share, share), :],
            s_sems,
            (distance - 1) * SLABS + k,
            device_of(to),
        )

    keep_factor = pltpu.make_async_copy(factor, columns_of(core), local_sems.at[0])
    keep_queries = pltpu.make_async_copy(
        queries, whole.at[:, at_multiple(blk * q_width, q_width)], local_sems.at[1]
    )
    keep_grads = pltpu.make_async_copy(
        train.at[:, at_multiple(chip * span, span)], grads, local_sems.at[2]
    )

    def exchange_queries(k):
        for distance in far_chips:
            a_copy(k, distance, chip).start()
        mixing[at_multiple(k * slab + chip * share, share), :] = whole[
            at_multiple(k * share, share), at_multiple(chip * span, span)
        ]

    def mix(k):
        for distance in far_chips:
            a_copy(k, distance, other_chip(-distance)).wait_recv()
        here = at_multiple(k * slab, slab)
        tile = min(256, n_rows)

        @pl.loop(0, n_rows // tile)
        def _(j):
            at = at_multiple(j * tile, tile)
            partial[here, at] = contract_last(mixing[here, :], weights[at, :]).astype(jnp.bfloat16)

        for distance in far_chips:
            b_copy(k, distance).start()

    def make_term(k):
        here = at_multiple(k * slab, slab)
        total = partial[here, :].astype(jnp.float32)
        for distance in far_chips:
            b_copy(k, distance).wait_recv()
            total = total + arrived[distance - 1, here, :].astype(jnp.float32)
        mixed[...] = total.astype(jnp.bfloat16)
        tile = min(512, span)

        @pl.loop(0, span // tile)
        def _(j):
            at = at_multiple(j * tile, tile)
            term[here, at] = jnp.dot(
                mixed[...], weights[:, at], preferred_element_type=jnp.float32
            ).astype(jnp.bfloat16)

    half = span // 2
    per_slab = half // CHUNK
    count = SLABS * per_slab
    flows = (
        (blk, {"blk": blk + 1}, {"blk": blk - 1}, 0, up_sum, up_share),
        (last - blk, {"blk": blk - 1}, {"blk": blk + 1}, half, down_sum, down_share),
    )

    def chunk(base, i, parts=1):
        start = base + (i % per_slab) // parts * parts * CHUNK
        return (
            at_multiple(i // per_slab * slab, slab),
            at_multiple(start, parts * CHUNK),
        )

    def sum_copy(flow, i, first=False):
        _, ahead, _, base, sum_sems, _ = flow
        here = chunk(base, i)
        return remote((term if first else sums).at[here], sums.at[here], sum_sems, i, ahead)

    def share_copy(flow, i):
        _, _, back, base, _, share_sems = flow
        part = precond.at[chunk(base, i)]
        return remote(part, part, share_sems, i, back)

    def add(flow, i):
        place, base = flow[0], flow[3]
        here = chunk(base, i)

        @pl.when(place == 0)
        def _():
            sum_copy(flow, i, True).start()

        @pl.when(place > 0)
        def _():
            sum_copy(flow, i).wait_recv()
            added = sums[here].astype(jnp.float32) + term[here].astype(jnp.float32)
            added = added.astype(jnp.bfloat16)

            @pl.when(place < last)
            def _():
                sums[here] = added
                sum_copy(flow, i).start()

            @pl.when(place == last)
            def _():
                precond[here] = added
                share_copy(flow, i).start()

    def use(flow, i):
        place, base = flow[0], flow[3]

        @pl.when(place < last)
        def _():
            share_copy(flow, i).wait_recv()
            pl.when(place > 0)(lambda: share_copy(flow, i).start())

        @pl.when(i % 2 == 1)
        def _():
            rows, cols = chunk(base, i, 2)
            found[rows, :] += contract_last(precond[rows, cols], grads[:, cols])

    def turn(t):
        for flow in flows:
            i = t - flow[0] * HOP
            pl.when((i >= 0) & (i < count))(functools.partial(add, flow, i))
        for flow in flows:
            i = t - (2 * last - flow[0]) * HOP
            pl.when((i >= 0) & (i < count))(functools.partial(use, flow, i))

    def send_found(k):
        for distance in far_chips:
            s_copy(k, distance).start()

    own_queries(0)
    f_copy(core).start()
    own_queries(1)
    keep_queries.start()
    keep_factor.start()
    keep_grads.start()
    found[...] = jnp.zeros_like(found)
    for k in range(SLABS):
        for far in range(1, n_blk):
            relay(k, far)
        if k + 2 < SLABS:
            own_queries(k + 2)
        if k == 0:
            keep_queries.wait()
        exchange_queries(k)
        if k == 1:
            keep_factor.wait()
            f_copy(1 - core).wait_recv()
        if 1 <= k < SLABS - 1:
            mix(k - 1)
        if 2 <= k < SLABS - 1:
            make_term(k - 2)
    keep_grads.wait()

    lag = 2 * last * HOP
    tasks = [
        (per_slab // 2, mix, SLABS - 2),
        (per_slab - 1, make_term, SLABS - 3),
        (per_slab + per_slab // 4, mix, SLABS - 1),
        (2 * per_slab - 2, make_term, SLABS - 2),
        (3 * per_slab - 3, make_term, SLABS - 1),
    ] + [((k + 1) * per_slab + lag, send_found, k) for k in range(SLABS)]
    begin = 0
    for end, task, k in sorted(tasks, key=lambda entry: entry[0]):
        if end > begin:
            pl.loop(begin, end)(turn)
            begin = end
        task(k)

    for k in range(SLABS):
        total = found[at_multiple(k * slab + chip * share, share), :]
        for distance in far_chips:
            s_copy(k, distance).wait_recv()
            total = total + others[distance - 1, k * share : (k + 1) * share, :]
        gathered[k * share : (k + 1) * share, :] = total
    scores[...] = gathered[...].T

    f_copy(core).wait_send()
    for k in range(SLABS):
        pl.when(blk < last)(lambda: q_own(k, True).wait_send())
        pl.when(blk > 0)(lambda: q_own(k, False).wait_send())
        for far in range(1, n_blk):
            pl.when((blk - far >= 0) & (blk < last))(
                lambda: q_relay(blk - far, k, True).wait_send()
            )
            pl.when((blk + far <= last) & (blk > 0))(
                lambda: q_relay(blk + far, k, False).wait_send()
            )
        for distance in far_chips:
            a_copy(k, distance, chip).wait_send()
            b_copy(k, distance).wait_send()
            s_copy(k, distance).wait_send()
    for flow in flows:
        place = flow[0]

        @pl.loop(0, count)
        def _(i):
            pl.when(place < last)(lambda: sum_copy(flow, i).wait_send())
            pl.when(place > 0)(lambda: share_copy(flow, i).wait_send())


def solution(mesh):
    n_blk, n_fac = mesh.shape["blk"], mesh.shape["fac"]
    chips = n_fac // CORES

    def shards(train_grads, queries, factor):
        examples, dims = train_grads.shape
        n_rows, width = factor.shape
        n_queries = queries.shape[0]
        span, many = CORES * width, chips * n_queries
        chunks = SLABS * (span // 2 // CHUNK)
        far = (chips - 1) * SLABS
        dma, bf16, f32 = pltpu.SemaphoreType.DMA, jnp.bfloat16, jnp.float32
        counts = [(n_blk + 2) * SLABS, n_blk * SLABS, 1, 1] + [far] * 6 + [chunks] * 8
        return pl.pallas_call(
            functools.partial(kernel, n_blk, n_fac),
            out_shape=jax.ShapeDtypeStruct((examples, n_queries), f32),
            in_specs=[pl.BlockSpec(memory_space=pl.ANY)] * 3,
            out_specs=pl.BlockSpec(memory_space=pltpu.VMEM),
            scratch_shapes=[
                pltpu.VMEM((n_rows, span), bf16),
                pltpu.VMEM((n_queries, dims), bf16),
                pltpu.VMEM((many, span), bf16),
                pltpu.VMEM((many, n_rows), bf16),
                pltpu.VMEM((chips - 1, many, n_rows), bf16),
                pltpu.VMEM((many // SLABS, n_rows), bf16),
                pltpu.VMEM((many, span), bf16),
                pltpu.VMEM((many, span), bf16),
                pltpu.VMEM((many, span), bf16),
                pltpu.VMEM((examples, span), bf16),
                pltpu.VMEM((many, examples), f32),
                pltpu.VMEM((chips - 1, n_queries, examples), f32),
                pltpu.VMEM((n_queries, examples), f32),
                dma((3,)),
            ]
            + [dma((size,)) for size in counts],
            compiler_params=pltpu.CompilerParams(
                collective_id=0, has_side_effects=True, vmem_limit_bytes=58 * 2**20
            ),
        )(train_grads, queries, factor)

    placed = (P(("grp", "blk"), None), P(("grp", "fac"), "blk"), P("blk", "fac"))
    return jax.shard_map(
        shards, mesh=mesh, in_specs=placed, out_specs=P(("grp", "blk"), "fac"), check_vma=False
    )
```

time: 492 us -> 206 us (0.42)
  waiting for transfers between devices: 433 us -> 0 us
  Pallas kernels: 0 us -> 204 us
  matrix products: 42.5 us -> 0 us
  between operations: 13.2 us -> 0.01 us
    all_gather x2 -> x0, waiting for transfers between devices: 286 us -> none  [the longest x1 202 us: shards(): factor_rows = lax.all_gather(factor, 'fac', axis=1, tiled=True)]
    pallas_call x0 -> x1, Pallas kernels: none -> 204 us  [shards(): pl.pallas_call(functools.partial(kernel, n_blk, n_fac), out_shape=jax.Sha...]
    reduce_scatter x1 -> x0, waiting for transfers between devices: 76.9 us -> none  [shards(): lax.psum_scatter(contract_cross(factor_rows, mixed_rows).astype(jnp.bfloa...]
    ppermute x3 -> x0, waiting for transfers between devices: 68.6 us -> none  [passed_along(): return lax.ppermute(value, axis, pairs)]
    dot_general x6 -> x0, matrix products: 42.5 us -> none  [the longest x1 16.4 us: contract_cross(): lax.dot_general(left, right, (((0,), (1,)), ((), ())), preferred_element_...]
  transfers between devices with their start and end apart: 6 -> 0, of which waited for: 6 -> 0; matrix products, arithmetic and copies ran while one was open for 1% -> 0% of each run, Pallas kernels for 0% -> 0%
where the time goes in v2:
time: 206 us
  Pallas kernels  204 us (99%)
    pallas_call x1, Pallas kernels, shards(): pl.pallas_call(functools.partial(kernel, n_blk, n_fac), out_shape=jax.Sha...  204 us

profile of v2, /device:TPU:0, one launch (start us, length us, event | category | flops | bytes accessed | tf_op | source)
XLA Modules:
  0.0 205.8 jit_solution(7344648735220782233)
XLA Ops:
  0.0 203.9 %shard_map.37 = f32[512,256]{1,0:T(8,128)} custom-call(bf16[512,8192]{1,0:T(8,128)(2,1)} %train.1, bf16[256,2048]{1,0:T(8,128)(2,1)} %queries.1, bf16[2048,2048]{1,0:T(8,128)(2,1)} %factor.1), custom_call_target="tpu_custom_call" | custom-call | tf_op jit(solution)/shard_map/pallas_call | solution.py:348
  203.9 1.9 copy.5

commit v3 on v2

--- a/solution.py
+++ b/solution.py
@@ -158,34 +158,47 @@
         ]
 
     def mix(k):
-        for distance in far_chips:
-            a_copy(k, distance, other_chip(-distance)).wait_recv()
         here = at_multiple(k * slab, slab)
         tile = min(256, n_rows)
 
-        @pl.loop(0, n_rows // tile)
-        def _(j):
+        def before():
+            for distance in far_chips:
+                a_copy(k, distance, other_chip(-distance)).wait_recv()
+
+        def one(j):
             at = at_multiple(j * tile, tile)
             partial[here, at] = contract_last(mixing[here, :], weights[at, :]).astype(jnp.bfloat16)
 
-        for distance in far_chips:
-            b_copy(k, distance).start()
+        def after():
+            for distance in far_chips:
+                b_copy(k, distance).start()
+
+        return before, one, n_rows // tile, after
 
     def make_term(k):
         here = at_multiple(k * slab, slab)
-        total = partial[here, :].astype(jnp.float32)
-        for distance in far_chips:
-            b_copy(k, distance).wait_recv()
-            total = total + arrived[distance - 1, here, :].astype(jnp.float32)
-        mixed[...] = total.astype(jnp.bfloat16)
         tile = min(512, span)
 
-        @pl.loop(0, span // tile)
-        def _(j):
+        def before():
+            total = partial[here, :].astype(jnp.float32)
+            for distance in far_chips:
+                b_copy(k, distance).wait_recv()
+                total = total + arrived[distance - 1, here, :].astype(jnp.float32)
+            mixed[...] = total.astype(jnp.bfloat16)
+
+        def one(j):
             at = at_multiple(j * tile, tile)
             term[here, at] = jnp.dot(
                 mixed[...], weights[:, at], preferred_element_type=jnp.float32
             ).astype(jnp.bfloat16)
+
+        return before, one, span // tile, lambda: None
+
+    def at_once(work):
+        before, one, tiles, after = work
+        before()
+        pl.loop(0, tiles)(one)
+        after()
 
     half = span // 2
     per_slab = half // CHUNK
@@ -280,25 +293,46 @@
             keep_factor.wait()
             f_copy(1 - core).wait_recv()
         if 1 <= k < SLABS - 1:
-            mix(k - 1)
+            at_once(mix(k - 1))
         if 2 <= k < SLABS - 1:
-            make_term(k - 2)
+            at_once(make_term(k - 2))
     keep_grads.wait()
 
+    def turns(begin, end, work=None):
+        if work is None:
+            pl.loop(begin, end)(turn)
+            return
+        before, one, tiles, after = work
+        each = -(-tiles // (end - begin))
+        before()
+
+        @pl.loop(begin, end)
+        def _(t):
+            turn(t)
+            for extra in range(each):
+                j = (t - begin) * each + extra
+                if each * (end - begin) == tiles:
+                    one(j)
+                else:
+                    pl.when(j < tiles)(functools.partial(one, j))
+
+        after()
+
     lag = 2 * last * HOP
-    tasks = [
-        (per_slab // 2, mix, SLABS - 2),
-        (per_slab - 1, make_term, SLABS - 3),
-        (per_slab + per_slab // 4, mix, SLABS - 1),
-        (2 * per_slab - 2, make_term, SLABS - 2),
-        (3 * per_slab - 3, make_term, SLABS - 1),
-    ] + [((k + 1) * per_slab + lag, send_found, k) for k in range(SLABS)]
-    begin = 0
-    for end, task, k in sorted(tasks, key=lambda entry: entry[0]):
+    part = per_slab // 2
+    turns(0, part, mix(SLABS - 2))
+    turns(part, 2 * part, make_term(SLABS - 3))
+    turns(2 * part, 3 * part, mix(SLABS - 1))
+    turns(3 * part, 4 * part, make_term(SLABS - 2))
+    turns(4 * part, 5 * part)
+    turns(5 * part, 6 * part, make_term(SLABS - 1))
+    begin = 6 * part
+    for k in range(SLABS):
+        end = (k + 1) * per_slab + lag
         if end > begin:
-            pl.loop(begin, end)(turn)
+            turns(begin, end)
             begin = end
-        task(k)
+        send_found(k)
 
     for k in range(SLABS):
         total = found[at_multiple(k * slab + chip * share, share), :]

time: 206 us -> 204 us (level)
  no operation moved by 1% of the time
where the time goes in v3:
time: 204 us
  Pallas kernels  202 us (99%)
    pallas_call x1, Pallas kernels, shards(): pl.pallas_call(functools.partial(kernel, n_blk, n_fac), out_shape=jax.Sha...  202 us

profile of v3, /device:TPU:0, one launch (start us, length us, event | category | flops | bytes accessed | tf_op | source)
XLA Modules:
  0.0 204.0 jit_solution(3592839079863713874)
XLA Ops:
  0.0 202.1 %shard_map.37 = f32[512,256]{1,0:T(8,128)} custom-call(bf16[512,8192]{1,0:T(8,128)(2,1)} %train.1, bf16[256,2048]{1,0:T(8,128)(2,1)} %queries.1, bf16[2048,2048]{1,0:T(8,128)(2,1)} %factor.1), custom_call_target="tpu_custom_call" | custom-call | tf_op jit(solution)/shard_map/pallas_call | solution.py:382
  202.1 1.9 copy.5
